TPU v7x, 32 devices: a whole 2x2x4 slice. The times are simulated.
32 devices in a mesh: ctx: 8 (over z, y), head: 4 (over x, core).
Axes of the slice: x: 2, y: 2, z: 4, core: 2. Of those that a mesh axis runs over, the one named last changes fastest.
Arguments:
- queries: bfloat16 [3072, 8, 128], P('ctx', 'head'), may hold values from -6 to 6
- key_rows: bfloat16 [3072, 128], P('ctx'), may hold values from -6 to 6
- value_rows: bfloat16 [3072, 128], P('ctx'), may hold values from -6 to 6
- grad_out: bfloat16 [3072, 8, 128], P('ctx', 'head'), may hold values from -6 to 6
- doc_lengths: int32 [64], replicated, may hold values from 1 to 2304, as said below
- block_pattern: int32 [24, 24], P('ctx'), may hold values from 0 to 1, as said below
Outputs:
- attn_out: bfloat16 [3072, 8, 128], P('ctx', 'head')
- grad_queries: bfloat16 [3072, 8, 128], P('ctx', 'head')
- grad_keys: bfloat16 [3072, 128], P('ctx')
- grad_values: bfloat16 [3072, 128], P('ctx')
Inputs may be any that keep to these rules, and one draw needn't show every extreme that they name: block_pattern[i, j] is 0 unless i // 3 - j // 3 is 0 or a positive power of two; it is 1 where i == j. `doc_lengths`: the lengths sum to 3072; the first document has exactly 2304 positions.
All inputs are finite; a program needn't handle non-finite values.
Results may differ from a plain program's by a relative error of at most 0.017.
Values may be sent and summed in bfloat16 or wider, within the bound.
A program may use at most 64 MiB of HBM per device.

v0:
```python
import math

import jax
import jax.numpy as jnp
from jax import lax
from jax.sharding import PartitionSpec as P

NEG_FILL = -1e30


def passed_along(value, axis, steps):
    count = lax.axis_size(axis)
    leading, last = (max(0, -steps), min(count, count - steps))
    return lax.ppermute(value, axis, [(source, source + steps) for source in range(leading, last)])


def doc_of(doc_ends, positions):
    return jnp.sum((doc_ends[None, :] <= positions[:, None]).astype(jnp.int32), axis=1)


def local(queries, key_rows, value_rows, grad_out, doc_lengths, block_pattern):
    tok_rows = queries.shape[0]
    local_heads = queries.shape[1]
    head_dim = key_rows.shape[1]
    block_count = block_pattern.shape[0]
    block_rows = tok_rows // block_count
    score_scale = 1.0 / math.sqrt(head_dim)
    ctx_width = lax.axis_size("ctx")
    level_count = ctx_width.bit_length() - 1
    own_index = lax.axis_index("ctx")
    offsets = jnp.arange(tok_rows, dtype=jnp.int32)
    query_pos = own_index * tok_rows + offsets
    doc_ends = jnp.cumsum(doc_lengths, dtype=jnp.int32)
    query_doc = doc_of(doc_ends, query_pos)
    partner_list = [own_index] + [own_index - (1 << bit_index) for bit_index in range(level_count)]
    active_list = [None] + [own_index >= 1 << bit_index for bit_index in range(level_count)]

    def level_mask(section_index):
        partner = jnp.maximum(partner_list[section_index], 0)
        key_pos = partner * tok_rows + offsets
        live_blocks = lax.dynamic_slice_in_dim(block_pattern, partner * block_count, block_count, 1)
        live_blocks = jnp.repeat(jnp.repeat(live_blocks, block_rows, axis=0), block_rows, axis=1)
        same_doc = query_doc[:, None] == doc_of(doc_ends, key_pos)[None, :]
        live = (live_blocks == 1) & same_doc & (key_pos[None, :] <= query_pos[:, None])
        if section_index == 0:
            return live
        return live & active_list[section_index]

    mask_list = [level_mask(section_index) for section_index in range(level_count + 1)]
    held_pairs = [(key_rows, value_rows)] + [
        passed_along((key_rows, value_rows), "ctx", 1 << bit_index)
        for bit_index in range(level_count)
    ]

    def run_level(section_index, level_work):
        if section_index == 0:
            return level_work()
        return level_work()

    score_list = []
    row_max = None
    row_total = None
    for section_index in range(level_count + 1):
        keys_here = held_pairs[section_index][0]
        live_mask = mask_list[section_index]

        def stat_work():
            raw_scores = (
                jnp.einsum("thd,ud->htu", queries, keys_here, preferred_element_type=jnp.float32)
                * score_scale
            )
            scores = jnp.where(live_mask[None], raw_scores, NEG_FILL)
            level_max = jnp.max(scores, axis=-1)
            level_total = jnp.sum(
                jnp.where(live_mask[None], jnp.exp(scores - level_max[..., None]), 0.0), axis=-1
            )
            return (scores, level_max, level_total)

        scores, level_max, level_total = run_level(section_index, stat_work)
        score_list.append(scores)
        if row_max is None:
            row_max = level_max
            row_total = level_total
        else:
            new_max = jnp.maximum(row_max, level_max)
            row_total = row_total * jnp.exp(row_max - new_max) + level_total * jnp.exp(
                level_max - new_max
            )
            row_max = new_max

    def probs_of(scores, live_mask):
        return jnp.where(
            live_mask[None], jnp.exp(scores - row_max[..., None]) / row_total[..., None], 0.0
        )

    out_acc = jnp.zeros((tok_rows, local_heads, head_dim), jnp.float32)
    for section_index in range(level_count + 1):
        values_here = held_pairs[section_index][1]
        live_mask = mask_list[section_index]
        scores = score_list[section_index]

        def output_work():
            probs_low = probs_of(scores, live_mask).astype(jnp.bfloat16)
            return jnp.einsum(
                "htu,ud->thd", probs_low, values_here, preferred_element_type=jnp.float32
            )

        out_acc = out_acc + run_level(section_index, output_work)
    attn_out = out_acc.astype(jnp.bfloat16)
    out_dot = jnp.sum(grad_out.astype(jnp.float32) * attn_out.astype(jnp.float32), axis=-1).T
    query_grad = jnp.zeros((tok_rows, local_heads, head_dim), jnp.float32)
    keys_grad = jnp.zeros((tok_rows, head_dim), jnp.float32)
    values_grad = jnp.zeros((tok_rows, head_dim), jnp.float32)
    for section_index in range(level_count + 1):
        keys_here, values_here = held_pairs[section_index]
        live_mask = mask_list[section_index]
        scores = score_list[section_index]

        def backward_work():
            probs = probs_of(scores, live_mask)
            probs_low = probs.astype(jnp.bfloat16)
            grad_prob = jnp.einsum(
                "thd,ud->htu", grad_out, values_here, preferred_element_type=jnp.float32
            )
            grad_score = (probs * (grad_prob - out_dot[..., None]) * score_scale).astype(
                jnp.bfloat16
            )
            part_query = jnp.einsum(
                "htu,ud->thd", grad_score, keys_here, preferred_element_type=jnp.float32
            )
            part_key = jnp.einsum(
                "htu,thd->ud", grad_score, queries, preferred_element_type=jnp.float32
            )
            part_value = jnp.einsum(
                "htu,thd->ud", probs_low, grad_out, preferred_element_type=jnp.float32
            )
            return (part_query, part_key, part_value)

        part_query, part_key, part_value = run_level(section_index, backward_work)
        query_grad = query_grad + part_query
        if section_index == 0:
            keys_grad = part_key
            values_grad = part_value
        else:
            back_key, back_value = passed_along(
                (part_key, part_value), "ctx", -(1 << section_index - 1)
            )
            keys_grad = keys_grad + back_key
            values_grad = values_grad + back_value
    keys_grad, values_grad = lax.psum((keys_grad, values_grad), "head")
    return (
        attn_out,
        query_grad.astype(jnp.bfloat16),
        keys_grad.astype(jnp.bfloat16),
        values_grad.astype(jnp.bfloat16),
    )


def solution(mesh):
    placed = (
        P("ctx", "head", None),
        P("ctx", None),
        P("ctx", None),
        P("ctx", "head", None),
        P(),
        P("ctx", None),
    )
    return jax.shard_map(
        local,
        mesh=mesh,
        in_specs=placed,
        out_specs=(P("ctx", "head", None), P("ctx", "head", None), P("ctx", None), P("ctx", None)),
        check_vma=False,
    )
```

profile of v0, /device:TPU:0, one launch (start us, length us, event | category | flops | bytes accessed | tf_op | source)
XLA Modules:
  0.0 85.7 jit_solution(11701172745937881411)
XLA Ops:
  0.7 1.1 %copy.99 = bf16[384,128]{0,1:T(8,128)(2,1)S(1)} copy(bf16[384,128]{1,0:T(8,128)(2,1)} %param.8) | data formatting | bytes 196608 | tf_op args[2]
  1.7 5.9 %collective-permute-start.5 = (bf16[384,128]{0,1:T(8,128)(2,1)S(1)}, bf16[384,128]{0,1:T(8,128)(2,1)S(1)}, u32[]{:S(2)}, u32[]{:S(2)}) collective-permute-start(bf16[384,128]{0,1:T(8,128)(2,1)S(1)} %copy.99), channel_id=1, source_target_pairs={{0,16},{4,20},{8,24},{12,28},{1,17},{5,21},{9,25},{13,29},{2,18},{... | collective-permute-start | bytes 294920 | tf_op jit(solution)/shard_map/ppermute | solution.py:14
  7.7 3.5 %collective-permute-start.4 = (bf16[384,128]{0,1:T(8,128)(2,1)S(1)}, bf16[384,128]{0,1:T(8,128)(2,1)S(1)}, u32[]{:S(2)}, u32[]{:S(2)}) collective-permute-start(bf16[384,128]{0,1:T(8,128)(2,1)S(1)} %copy.99), channel_id=1, source_target_pairs={{0,8},{4,12},{8,16},{12,20},{16,24},{20,28},{1,9},{5,13},{9,17},{1... | collective-permute-start | bytes 294920 | tf_op jit(solution)/shard_map/ppermute | solution.py:14
  11.2 3.4 %collective-permute-start.3 = (bf16[384,128]{0,1:T(8,128)(2,1)S(1)}, bf16[384,128]{0,1:T(8,128)(2,1)S(1)}, u32[]{:S(2)}, u32[]{:S(2)}) collective-permute-start(bf16[384,128]{0,1:T(8,128)(2,1)S(1)} %copy.99), channel_id=1, source_target_pairs={{0,4},{4,8},{8,12},{12,16},{16,20},{20,24},{24,28},{1,5},{5,9},{9,... | collective-permute-start | bytes 294920 | tf_op jit(solution)/shard_map/ppermute | solution.py:14
  14.6 1.9 %collective-permute-start = (bf16[384,128]{1,0:T(8,128)(2,1)}, bf16[384,128]{1,0:T(8,128)(2,1)S(1)}, u32[]{:S(2)}, u32[]{:S(2)}) collective-permute-start(bf16[384,128]{1,0:T(8,128)(2,1)} %param.7), channel_id=1, source_target_pairs={{0,4},{4,8},{8,12},{12,16},{16,20},{20,24},{24,28},{1,5},{5,9},{9,... | collective-permute-start | bytes 294920 | tf_op jit(solution)/shard_map/ppermute | solution.py:14
  16.5 1.9 %collective-permute-start.1 = (bf16[384,128]{1,0:T(8,128)(2,1)}, bf16[384,128]{1,0:T(8,128)(2,1)S(1)}, u32[]{:S(2)}, u32[]{:S(2)}) collective-permute-start(bf16[384,128]{1,0:T(8,128)(2,1)} %param.7), channel_id=1, source_target_pairs={{0,8},{4,12},{8,16},{12,20},{16,24},{20,28},{1,9},{5,13},{9,17},{1... | collective-permute-start | bytes 294920 | tf_op jit(solution)/shard_map/ppermute | solution.py:14
  18.5 0.9 %dynamic-slice_compare_fusion.2 = (pred[3,3]{1,0:T(4,128)(4,1)S(1)}, pred[3,3]{1,0:T(4,128)(4,1)S(1)}, pred[3,3]{1,0:T(4,128)(4,1)S(1)}, pred[3,3]{1,0:T(4,128)(4,1)S(1)}) fusion(s32[3,24]{1,0:T(4,128)} %param.11, s32[]{:T(128)S(6)} %select_n.55, s32[]{:T(128)S(6)} %select_n.53, s32[]{:T(128)S(6)} %select_n.59, s32[]{:T(128)S(6)} %select_n.57), kind=kLoop, calls=%fused_computation.131 | loop fusion | flops 36 | bytes 196 | tf_op jit(solution)/shard_map/eq | solution.py:44
  21.1 1.1 %copy.106 = bf16[384,2,128]{0,2,1:T(8,128)(2,1)S(1)} copy(bf16[384,2,128]{2,1,0:T(2,128)(2,1)} %param.9) | data formatting | bytes 393216 | tf_op args[3]
  22.4 1.0 %fusion.41 = (pred[384,384]{0,1:T(8,128)(4,1)S(1)}, pred[384,384]{0,1:T(8,128)(4,1)S(1)}, pred[384,384]{0,1:T(8,128)(4,1)S(1)}, pred[384,384]{0,1:T(8,128)(4,1)S(1)}) fusion(s32[384]{0:T(512)S(1)} %iota_add_fusion.4, s32[384]{0:T(512)S(1)} %get-tuple-element.20, s32[384]{0:T(512)S(1)} %get-tuple-element.47, s32[384]{0:T(512)S(1)} %get-tuple-element.18, ...), kind=kLoop, calls=%fused_computation.72 | loop fusion | flops 2801664 | bytes 609795 | tf_op jit(solution)/shard_map/and | solution.py:47
  24.1 1.3 %collective-permute-start.2 = (bf16[384,128]{1,0:T(8,128)(2,1)S(1)}, bf16[384,128]{1,0:T(8,128)(2,1)S(1)}, u32[]{:S(2)}, u32[]{:S(2)}) collective-permute-start(bf16[384,128]{1,0:T(8,128)(2,1)S(1)} %copy-done.4), channel_id=1, source_target_pairs={{0,16},{4,20},{8,24},{12,28},{1,17},{5,21},{9,25},{13,29},{2,18},{... | collective-permute-start | bytes 294920 | tf_op jit(solution)/shard_map/ppermute | solution.py:14
  26.7 0.9 %collective-permute-done.2 = bf16[384,128]{1,0:T(8,128)(2,1)S(1)} collective-permute-done((bf16[384,128]{1,0:T(8,128)(2,1)S(1)}, bf16[384,128]{1,0:T(8,128)(2,1)S(1)}, u32[]{:S(2)}, u32[]{:S(2)}) %collective-permute-start.2) | collective-permute-done | bytes 98336 | tf_op jit(solution)/shard_map/ppermute | solution.py:14
  28.2 1.1 %convolution_bitcast_fusion.4 = f32[384,128]{1,0:T(8,128)} fusion(bf16[384,2,128]{0,2,1:T(8,128)(2,1)S(1)} %copy.106, f32[2,384,384]{1,2,0:T(8,128)S(1)} %get-tuple-element.36, f32[2,384]{1,0:T(2,128)S(1)} %get-tuple-element.23, f32[2,384]{1,0:T(2,128)S(1)} %get-tuple-element.24, pred[384,384]{0,1:T(8,128)(4,1)S(1)} %get-tuple-element.29), kind=kOutput, calls=%fused_computation.48 | convolution fusion | flops 76677120 | bytes 1726464 | tf_op jit(solution)/shard_map/htu,thd->ud/dot_general | solution.py:134
  29.3 1.1 %convolution_bitcast_fusion.5 = f32[384,128]{1,0:T(8,128)} fusion(bf16[384,2,128]{0,2,1:T(8,128)(2,1)S(1)} %copy.106, f32[2,384,384]{1,2,0:T(8,128)S(1)} %get-tuple-element.38, f32[2,384]{1,0:T(2,128)S(1)} %get-tuple-element.23, f32[2,384]{1,0:T(2,128)S(1)} %get-tuple-element.24, pred[384,384]{0,1:T(8,128)(4,1)S(1)} %get-tuple-element.28), kind=kOutput, calls=%fused_computation.49 | convolution fusion | flops 76677120 | bytes 1726464 | tf_op jit(solution)/shard_map/htu,thd->ud/dot_general | solution.py:134
  30.4 1.1 %convolution_bitcast_fusion.6 = f32[384,128]{1,0:T(8,128)} fusion(bf16[384,2,128]{0,2,1:T(8,128)(2,1)S(1)} %copy.106, f32[2,384,384]{1,2,0:T(8,128)S(1)} %get-tuple-element.42, f32[2,384]{1,0:T(2,128)S(1)} %get-tuple-element.23, f32[2,384]{1,0:T(2,128)S(1)} %get-tuple-element.24, pred[384,384]{0,1:T(8,128)(4,1)S(1)} %get-tuple-element.27), kind=kOutput, calls=%fused_computation.50 | convolution fusion | flops 76677120 | bytes 1726464 | tf_op jit(solution)/shard_map/htu,thd->ud/dot_general | solution.py:134
  31.9 1.3 %collective-permute-start.9 = (f32[384,128]{1,0:T(8,128)}, f32[384,128]{1,0:T(8,128)}, u32[]{:S(2)}, u32[]{:S(2)}) collective-permute-start(f32[384,128]{1,0:T(8,128)} %convolution_bitcast_fusion.6), channel_id=1, source_target_pairs={{4,0},{8,4},{12,8},{16,12},{20,16},{24,20},{28,24},{5,1},{9,5},{13... | collective-permute-start | bytes 589832 | tf_op jit(solution)/shard_map/ppermute | solution.py:14
  33.2 1.3 %collective-permute-start.10 = (f32[384,128]{1,0:T(8,128)}, f32[384,128]{1,0:T(8,128)}, u32[]{:S(2)}, u32[]{:S(2)}) collective-permute-start(f32[384,128]{1,0:T(8,128)} %convolution_bitcast_fusion.5), channel_id=1, source_target_pairs={{8,0},{12,4},{16,8},{20,12},{24,16},{28,20},{9,1},{13,5},{17,9},{2... | collective-permute-start | bytes 589832 | tf_op jit(solution)/shard_map/ppermute | solution.py:14
  34.5 1.3 %collective-permute-start.11 = (f32[384,128]{1,0:T(8,128)}, f32[384,128]{1,0:T(8,128)}, u32[]{:S(2)}, u32[]{:S(2)}) collective-permute-start(f32[384,128]{1,0:T(8,128)} %convolution_bitcast_fusion.4), channel_id=1, source_target_pairs={{16,0},{20,4},{24,8},{28,12},{17,1},{21,5},{25,9},{29,13},{18,2},{... | collective-permute-start | bytes 589832 | tf_op jit(solution)/shard_map/ppermute | solution.py:14
  36.9 1.1 %multiply_reduce_fusion = (f32[384,2]{0,1:T(2,128)S(1)}, bf16[384,2,128]{0,2,1:T(8,128)(2,1)}) fusion(bf16[384,2,128]{0,2,1:T(8,128)(2,1)S(1)} %copy.106, f32[2,384,128]{1,2,0:T(8,128)S(1)} %fusion.44, f32[2,384,128]{1,2,0:T(8,128)S(1)} %convolution_add_fusion.1, f32[2,384]{1,0:T(2,128)S(1)} %get-tuple-element.23, ...), kind=kOutput, calls=%fused_computation.75 | convolution fusion | flops 77364480 | bytes 2614272 | tf_op jit(solution)/shard_map/htu,ud->thd/dot_general | solution.py:104
  39.4 1.0 %convolution_bitcast_fusion.9 = f32[384,128]{1,0:T(8,128)} fusion(bf16[2,384,384]{1,2,0:T(8,128)(2,1)S(1)} %fusion.22, bf16[384,2,128]{2,1,0:T(2,128)(2,1)S(1)} %copy-done), kind=kOutput, calls=%fused_computation.53 | convolution fusion | flops 75497472 | bytes 983040 | tf_op jit(solution)/shard_map/htu,thd->ud/dot_general | solution.py:131
  40.5 1.5 %fusion.21 = bf16[2,384,384]{1,2,0:T(8,128)(2,1)S(1)} fusion(bf16[384,2,128]{0,2,1:T(8,128)(2,1)} %copy-done.2, f32[2,384]{1,0:T(2,128)S(1)} %bitcast.209, bf16[384,128]{0,1:T(8,128)(2,1)S(1)} %copy-done.14, f32[2,384]{1,0:T(2,128)S(1)} %get-tuple-element.23, f32[2,384,384]{1,2,0:T(8,128)S(1)} %get-tuple-element.42, f32[2,384]{1,0:T(2,128)S(1)} %get-tuple-element.24, ...), kind=kOutput, calls=%fused_computation.29 | convolution fusion | flops 77561856 | bytes 2221056 | tf_op jit(solution)/shard_map/thd,ud->htu/dot_general | solution.py:122
  41.9 1.0 %convolution_bitcast_fusion.10 = f32[384,128]{1,0:T(8,128)} fusion(bf16[2,384,384]{1,2,0:T(8,128)(2,1)S(1)} %fusion.21, bf16[384,2,128]{2,1,0:T(2,128)(2,1)S(1)} %copy-done), kind=kOutput, calls=%fused_computation.54 | convolution fusion | flops 75497472 | bytes 983040 | tf_op jit(solution)/shard_map/htu,thd->ud/dot_general | solution.py:131
  42.9 1.8 %copy.125 = bf16[384,2,128]{2,1,0:T(2,128)(2,1)} copy(bf16[384,2,128]{0,2,1:T(8,128)(2,1)} %get-tuple-element.44) | data formatting | bytes 393216
  44.7 1.3 %collective-permute-start.6 = (f32[384,128]{1,0:T(8,128)}, f32[384,128]{1,0:T(8,128)S(1)}, u32[]{:S(2)}, u32[]{:S(2)}) collective-permute-start(f32[384,128]{1,0:T(8,128)} %convolution_bitcast_fusion.10), channel_id=1, source_target_pairs={{4,0},{8,4},{12,8},{16,12},{20,16},{24,20},{28,24},{5,1},{9,5},{13... | collective-permute-start | bytes 589832 | tf_op jit(solution)/shard_map/ppermute | solution.py:14
  46.0 1.3 %collective-permute-start.7 = (f32[384,128]{1,0:T(8,128)}, f32[384,128]{1,0:T(8,128)S(1)}, u32[]{:S(2)}, u32[]{:S(2)}) collective-permute-start(f32[384,128]{1,0:T(8,128)} %convolution_bitcast_fusion.9), channel_id=1, source_target_pairs={{8,0},{12,4},{16,8},{20,12},{24,16},{28,20},{9,1},{13,5},{17,9},{2... | collective-permute-start | bytes 589832 | tf_op jit(solution)/shard_map/ppermute | solution.py:14
  47.7 2.0 %fusion.23 = bf16[2,384,384]{1,2,0:T(8,128)(2,1)S(1)} fusion(bf16[384,2,128]{0,2,1:T(8,128)(2,1)} %copy-done.2, f32[2,384]{1,0:T(2,128)S(1)} %bitcast.210, bf16[384,128]{0,1:T(8,128)(2,1)} %copy-done.12, f32[2,384]{1,0:T(2,128)S(1)} %get-tuple-element.23, f32[2,384,384]{1,2,0:T(8,128)} %copy-done.1, f32[2,384]{1,0:T(2,128)S(1)} %get-tuple-element.24, ...), kind=kOutput, calls=%fused_computation.31 | convolution fusion | flops 77561856 | bytes 2221056 | tf_op jit(solution)/shard_map/thd,ud->htu/dot_general | solution.py:122
  51.0 0.9 %copy.126 = bf16[384,2,128]{2,1,0:T(2,128)(2,1)} copy(bf16[384,2,128]{2,0,1:T(8,128)(2,1)S(1)} %fusion.28) | data formatting | bytes 393216
  52.2 1.3 %collective-permute-start.8 = (f32[384,128]{1,0:T(8,128)S(1)}, f32[384,128]{1,0:T(8,128)S(1)}, u32[]{:S(2)}, u32[]{:S(2)}) collective-permute-start(f32[384,128]{1,0:T(8,128)S(1)} %convolution_bitcast_fusion.8), channel_id=1, source_target_pairs={{16,0},{20,4},{24,8},{28,12},{17,1},{21,5},{25,9},{29,13},{18,2},{... | collective-permute-start | bytes 589832 | tf_op jit(solution)/shard_map/ppermute | solution.py:14
  53.5 1.9 %collective-permute-done.11 = f32[384,128]{1,0:T(8,128)} collective-permute-done((f32[384,128]{1,0:T(8,128)}, f32[384,128]{1,0:T(8,128)}, u32[]{:S(2)}, u32[]{:S(2)}) %collective-permute-start.11) | collective-permute-done | bytes 196640 | tf_op jit(solution)/shard_map/ppermute | solution.py:14
  55.3 1.5 %fusion.35 = f32[384,128]{1,0:T(8,128)S(1)} fusion(f32[384,128]{1,0:T(8,128)} %collective-permute-done.11, f32[384,128]{1,0:T(8,128)} %collective-permute-done.10, f32[384,128]{1,0:T(8,128)} %collective-permute-done.9, bf16[384,2,128]{0,2,1:T(8,128)(2,1)S(1)} %copy-done.3, f32[2,384,384]{1,2,0:T(8,128)S(1)} %get-tuple-element.40, ...), kind=kOutput, calls=%fused_computation.63 | convolution fusion | flops 76824576 | bytes 2316288 | tf_op jit(solution)/shard_map/htu,thd->ud/dot_general | solution.py:134
  56.9 3.7 %collective-permute-done.7 = f32[384,128]{1,0:T(8,128)S(1)} collective-permute-done((f32[384,128]{1,0:T(8,128)}, f32[384,128]{1,0:T(8,128)S(1)}, u32[]{:S(2)}, u32[]{:S(2)}) %collective-permute-start.7) | collective-permute-done | bytes 196640 | tf_op jit(solution)/shard_map/ppermute | solution.py:14
  60.5 9.7 %collective-permute-done.8 = f32[384,128]{1,0:T(8,128)S(1)} collective-permute-done((f32[384,128]{1,0:T(8,128)S(1)}, f32[384,128]{1,0:T(8,128)S(1)}, u32[]{:S(2)}, u32[]{:S(2)}) %collective-permute-start.8) | collective-permute-done | bytes 196640 | tf_op jit(solution)/shard_map/ppermute | solution.py:14
  70.5 15.2 %all-reduce.2 = (bf16[384,128]{1,0:T(8,128)(2,1)}, bf16[384,128]{1,0:T(8,128)(2,1)}) all-reduce(f32[384,128]{1,0:T(8,128)S(1)} %fusion.32, f32[384,128]{1,0:T(8,128)S(1)} %fusion.35), channel_id=1, replica_groups=mesh['ctx'=8,'head'=4] {'head'}, use_global_device_ids=true, to_apply=%region_15.16 | all-reduce | flops 98304 | bytes 589824 | tf_op jit(solution)/shard_map/psum | solution.py:150
  (80 shorter events, 9.6 us)
Async XLA Ops:
  0.6 22.8 %copy-start = (bf16[384,2,128]{2,1,0:T(2,128)(2,1)S(1)}, bf16[384,2,128]{2,1,0:T(2,128)(2,1)}, u32[]{:S(2)}) copy-start(bf16[384,2,128]{2,1,0:T(2,128)(2,1)} %param.6) | copy-start | bytes 589828
  0.6 22.8 %copy-start.4 = (bf16[384,128]{1,0:T(8,128)(2,1)S(1)}, bf16[384,128]{1,0:T(8,128)(2,1)}, u32[]{:S(2)}) copy-start(bf16[384,128]{1,0:T(8,128)(2,1)} %param.7) | copy-start | bytes 294916
  1.7 34.5 %collective-permute-start.5 = (bf16[384,128]{0,1:T(8,128)(2,1)S(1)}, bf16[384,128]{0,1:T(8,128)(2,1)S(1)}, u32[]{:S(2)}, u32[]{:S(2)}) collective-permute-start(bf16[384,128]{0,1:T(8,128)(2,1)S(1)} %copy.99), channel_id=1, source_target_pairs={{0,16},{4,20},{8,24},{12,28},{1,17},{5,21},{9,25},{13,29},{2,18},{... | collective-permute-start | bytes 294920 | tf_op jit(solution)/shard_map/ppermute | solution.py:14
  7.7 29.2 %collective-permute-start.4 = (bf16[384,128]{0,1:T(8,128)(2,1)S(1)}, bf16[384,128]{0,1:T(8,128)(2,1)S(1)}, u32[]{:S(2)}, u32[]{:S(2)}) collective-permute-start(bf16[384,128]{0,1:T(8,128)(2,1)S(1)} %copy.99), channel_id=1, source_target_pairs={{0,8},{4,12},{8,16},{12,20},{16,24},{20,28},{1,9},{5,13},{9,17},{1... | collective-permute-start | bytes 294920 | tf_op jit(solution)/shard_map/ppermute | solution.py:14
  11.2 23.3 %collective-permute-start.3 = (bf16[384,128]{0,1:T(8,128)(2,1)S(1)}, bf16[384,128]{0,1:T(8,128)(2,1)S(1)}, u32[]{:S(2)}, u32[]{:S(2)}) collective-permute-start(bf16[384,128]{0,1:T(8,128)(2,1)S(1)} %copy.99), channel_id=1, source_target_pairs={{0,4},{4,8},{8,12},{12,16},{16,20},{20,24},{24,28},{1,5},{5,9},{9,... | collective-permute-start | bytes 294920 | tf_op jit(solution)/shard_map/ppermute | solution.py:14
  14.6 9.5 %collective-permute-start = (bf16[384,128]{1,0:T(8,128)(2,1)}, bf16[384,128]{1,0:T(8,128)(2,1)S(1)}, u32[]{:S(2)}, u32[]{:S(2)}) collective-permute-start(bf16[384,128]{1,0:T(8,128)(2,1)} %param.7), channel_id=1, source_target_pairs={{0,4},{4,8},{8,12},{12,16},{16,20},{20,24},{24,28},{1,5},{5,9},{9,... | collective-permute-start | bytes 294920 | tf_op jit(solution)/shard_map/ppermute | solution.py:14
  16.5 9.5 %collective-permute-start.1 = (bf16[384,128]{1,0:T(8,128)(2,1)}, bf16[384,128]{1,0:T(8,128)(2,1)S(1)}, u32[]{:S(2)}, u32[]{:S(2)}) collective-permute-start(bf16[384,128]{1,0:T(8,128)(2,1)} %param.7), channel_id=1, source_target_pairs={{0,8},{4,12},{8,16},{12,20},{16,24},{20,28},{1,9},{5,13},{9,17},{1... | collective-permute-start | bytes 294920 | tf_op jit(solution)/shard_map/ppermute | solution.py:14
  22.2 16.3 %copy-start.2 = (bf16[384,2,128]{0,2,1:T(8,128)(2,1)}, bf16[384,2,128]{0,2,1:T(8,128)(2,1)S(1)}, u32[]{:S(2)}) copy-start(bf16[384,2,128]{0,2,1:T(8,128)(2,1)S(1)} %copy.106) | copy-start | bytes 589828
  24.1 1.9 %copy-start.5 = (bf16[384,128]{1,0:T(8,128)(2,1)}, bf16[384,128]{1,0:T(8,128)(2,1)S(1)}, u32[]{:S(2)}) copy-start(bf16[384,128]{1,0:T(8,128)(2,1)S(1)} %collective-permute-done) | copy-start | bytes 294916
  24.1 3.5 %collective-permute-start.2 = (bf16[384,128]{1,0:T(8,128)(2,1)S(1)}, bf16[384,128]{1,0:T(8,128)(2,1)S(1)}, u32[]{:S(2)}, u32[]{:S(2)}) collective-permute-start(bf16[384,128]{1,0:T(8,128)(2,1)S(1)} %copy-done.4), channel_id=1, source_target_pairs={{0,16},{4,20},{8,24},{12,28},{1,17},{5,21},{9,25},{13,29},{2,18},{... | collective-permute-start | bytes 294920 | tf_op jit(solution)/shard_map/ppermute | solution.py:14
  26.0 0.6 copy-start.7
  27.6 0.6 copy-start.9
  27.9 8.3 %copy-start.1 = (f32[2,384,384]{1,2,0:T(8,128)}, f32[2,384,384]{1,2,0:T(8,128)S(1)}, u32[]{:S(2)}) copy-start(f32[2,384,384]{1,2,0:T(8,128)S(1)} %get-tuple-element.36) | copy-start | bytes 3538948
  30.4 1.1 %copy-start.11 = (bf16[384,128]{1,0:T(8,128)(2,1)S(1)}, bf16[384,128]{1,0:T(8,128)(2,1)}, u32[]{:S(2)}) copy-start(bf16[384,128]{1,0:T(8,128)(2,1)} %param.8) | copy-start | bytes 294916
  31.9 20.3 %collective-permute-start.9 = (f32[384,128]{1,0:T(8,128)}, f32[384,128]{1,0:T(8,128)}, u32[]{:S(2)}, u32[]{:S(2)}) collective-permute-start(f32[384,128]{1,0:T(8,128)} %convolution_bitcast_fusion.6), channel_id=1, source_target_pairs={{4,0},{8,4},{12,8},{16,12},{20,16},{24,20},{28,24},{5,1},{9,5},{13... | collective-permute-start | bytes 589832 | tf_op jit(solution)/shard_map/ppermute | solution.py:14
  33.2 20.3 %collective-permute-start.10 = (f32[384,128]{1,0:T(8,128)}, f32[384,128]{1,0:T(8,128)}, u32[]{:S(2)}, u32[]{:S(2)}) collective-permute-start(f32[384,128]{1,0:T(8,128)} %convolution_bitcast_fusion.5), channel_id=1, source_target_pairs={{8,0},{12,4},{16,8},{20,12},{24,16},{28,20},{9,1},{13,5},{17,9},{2... | collective-permute-start | bytes 589832 | tf_op jit(solution)/shard_map/ppermute | solution.py:14
  34.5 1.7 %copy-start.13 = (bf16[384,128]{0,1:T(8,128)(2,1)}, bf16[384,128]{0,1:T(8,128)(2,1)S(1)}, u32[]{:S(2)}) copy-start(bf16[384,128]{0,1:T(8,128)(2,1)S(1)} %collective-permute-done.3) | copy-start | bytes 294916
  34.5 20.9 %collective-permute-start.11 = (f32[384,128]{1,0:T(8,128)}, f32[384,128]{1,0:T(8,128)}, u32[]{:S(2)}, u32[]{:S(2)}) collective-permute-start(f32[384,128]{1,0:T(8,128)} %convolution_bitcast_fusion.4), channel_id=1, source_target_pairs={{16,0},{20,4},{24,8},{28,12},{17,1},{21,5},{25,9},{29,13},{18,2},{... | collective-permute-start | bytes 589832 | tf_op jit(solution)/shard_map/ppermute | solution.py:14
  36.2 0.6 copy-start.12
  36.9 1.1 %copy-start.15 = (bf16[384,128]{0,1:T(8,128)(2,1)}, bf16[384,128]{0,1:T(8,128)(2,1)S(1)}, u32[]{:S(2)}) copy-start(bf16[384,128]{0,1:T(8,128)(2,1)S(1)} %collective-permute-done.4) | copy-start | bytes 294916
  38.0 0.9 %copy-start.16 = (bf16[384,128]{0,1:T(8,128)(2,1)S(1)}, bf16[384,128]{0,1:T(8,128)(2,1)}, u32[]{:S(2)}) copy-start(bf16[384,128]{0,1:T(8,128)(2,1)} %copy-done.15) | copy-start | bytes 294916
  38.9 1.6 %copy-start.14 = (bf16[384,128]{0,1:T(8,128)(2,1)S(1)}, bf16[384,128]{0,1:T(8,128)(2,1)}, u32[]{:S(2)}) copy-start(bf16[384,128]{0,1:T(8,128)(2,1)} %copy-done.13) | copy-start | bytes 294916
  44.7 12.2 %collective-permute-start.6 = (f32[384,128]{1,0:T(8,128)}, f32[384,128]{1,0:T(8,128)S(1)}, u32[]{:S(2)}, u32[]{:S(2)}) collective-permute-start(f32[384,128]{1,0:T(8,128)} %convolution_bitcast_fusion.10), channel_id=1, source_target_pairs={{4,0},{8,4},{12,8},{16,12},{20,16},{24,20},{28,24},{5,1},{9,5},{13... | collective-permute-start | bytes 589832 | tf_op jit(solution)/shard_map/ppermute | solution.py:14
  46.0 14.5 %collective-permute-start.7 = (f32[384,128]{1,0:T(8,128)}, f32[384,128]{1,0:T(8,128)S(1)}, u32[]{:S(2)}, u32[]{:S(2)}) collective-permute-start(f32[384,128]{1,0:T(8,128)} %convolution_bitcast_fusion.9), channel_id=1, source_target_pairs={{8,0},{12,4},{16,8},{20,12},{24,16},{28,20},{9,1},{13,5},{17,9},{2... | collective-permute-start | bytes 589832 | tf_op jit(solution)/shard_map/ppermute | solution.py:14
  47.7 2.0 %copy-start.10 = (bf16[384,128]{1,0:T(8,128)(2,1)S(1)}, bf16[384,128]{1,0:T(8,128)(2,1)}, u32[]{:S(2)}) copy-start(bf16[384,128]{1,0:T(8,128)(2,1)} %copy-done.9) | copy-start | bytes 294916
  47.7 2.4 %copy-start.6 = (bf16[384,128]{1,0:T(8,128)(2,1)S(1)}, bf16[384,128]{1,0:T(8,128)(2,1)}, u32[]{:S(2)}) copy-start(bf16[384,128]{1,0:T(8,128)(2,1)} %copy-done.5) | copy-start | bytes 294916
  49.7 0.9 %copy-start.8 = (bf16[384,128]{1,0:T(8,128)(2,1)S(1)}, bf16[384,128]{1,0:T(8,128)(2,1)}, u32[]{:S(2)}) copy-start(bf16[384,128]{1,0:T(8,128)(2,1)} %copy-done.7) | copy-start | bytes 294916
  50.6 4.8 %copy-start.3 = (bf16[384,2,128]{0,2,1:T(8,128)(2,1)S(1)}, bf16[384,2,128]{0,2,1:T(8,128)(2,1)}, u32[]{:S(2)}) copy-start(bf16[384,2,128]{0,2,1:T(8,128)(2,1)} %copy-done.2) | copy-start | bytes 589828
  52.2 18.0 %collective-permute-start.8 = (f32[384,128]{1,0:T(8,128)S(1)}, f32[384,128]{1,0:T(8,128)S(1)}, u32[]{:S(2)}, u32[]{:S(2)}) collective-permute-start(f32[384,128]{1,0:T(8,128)S(1)} %convolution_bitcast_fusion.8), channel_id=1, source_target_pairs={{16,0},{20,4},{24,8},{28,12},{17,1},{21,5},{25,9},{29,13},{18,2},{... | collective-permute-start | bytes 589832 | tf_op jit(solution)/shard_map/ppermute | solution.py:14
where the time goes:
time: 86.4 us; the launch traced here: 85.7 us
  starting transfers between devices  25.7 us (30%)
  matrix products  17.1 us (20%)
  waiting for transfers between devices  16.1 us (19%)
  blocking collectives  15.2 us (18%)
  local copies, waits for them, and re-layouts  7.09 us (8%)
  other arithmetic  3.29 us (4%)
  between operations  1.16 us (1%)
    ppermute x12, starting transfers between devices, passed_along(): lax.ppermute(value, axis, [(source, source + steps) for source in range(l...  25.7 us
    ppermute x12, waiting for transfers between devices, passed_along(): lax.ppermute(value, axis, [(source, source + steps) for source in range(l...  16.1 us
    psum x1, blocking collectives, local(): keys_grad, values_grad = lax.psum((keys_grad, values_grad), 'head')  15.2 us
    unnamed x42, local copies, waits for them, and re-layouts  5.9 us
    dot_general x4, matrix products, backward_work(): jnp.einsum('htu,thd->ud', probs_low, grad_out, preferred_element_type=jnp...  4.71 us
    dot_general x4, matrix products, backward_work(): jnp.einsum('thd,ud->htu', grad_out, values_here, preferred_element_type=j...  4.49 us
    dot_general x4, matrix products, backward_work(): jnp.einsum('htu,thd->ud', grad_score, queries, preferred_element_type=jnp...  2.64 us
    dot_general x4, matrix products, output_work(): jnp.einsum('htu,ud->thd', probs_low, values_here, preferred_element_type=...  2.35 us
  transfers between devices with their start and end apart: 12, of which 4 were waited for; matrix products, arithmetic and copies ran while one was open for 30% of the time, Pallas kernels for 0%

commit v1 on v0

v1 whole, which is shorter than its diff:
```python
import functools
import math

import jax
import jax.numpy as jnp
from jax import lax
from jax.experimental import pallas as pl
from jax.experimental.pallas import tpu as pltpu
from jax.sharding import PartitionSpec as P

NEG_FILL = -1e30
FAR = 1e9
MESH = pl.DeviceIdType.MESH
F32 = jnp.float32
LOW = jnp.bfloat16


def dot(a, b, dim_a, dim_b):
    return lax.dot_general(
        a, b, (((dim_a,), (dim_b,)), ((), ())), preferred_element_type=F32
    )


def remote(src, dst, sent, landed, ctx, head):
    return pltpu.make_async_remote_copy(
        src_ref=src,
        dst_ref=dst,
        send_sem=sent,
        recv_sem=landed,
        device_id=(ctx, head),
        device_id_type=MESH,
    )


def kernel(
    ctx_width, head_width, group, pattern, lengths, q_in, k_in, v_in, g_in,
    o_out, dq_out, dk_out, dv_out,
    kv, q, g, e, f, dp, top, tot, acc, mean, low_buf, dq_buf,
    keep, swap_out, swap_in, flow_out, flow_in, total, final,
    load_sem, store_sem, kv_sent, kv_landed, pair_sent, pair_landed,
    swap_sent, swap_landed, flow_sent, flow_landed, fin_sent, fin_landed,
):
    tok_rows, dim = k_in.shape
    rows = q_in.shape[0]
    block_count = pattern.shape[0]
    block = tok_rows // block_count
    block_q = block * group
    sections = kv.shape[0]
    parts = head_width // 2
    part_rows = tok_rows // parts
    scale = 1.0 / math.sqrt(dim)
    first_doc = 3 * ctx_width // 4
    c = lax.axis_index("ctx")
    h = lax.axis_index("head")
    kind = lax.rem(h, 2)
    x = lax.div(h, 2)
    sibling = h + 1 - 2 * kind
    gaps = [0] + [1 << bit for bit in range(sections - 1)]

    def sends(s):
        d = gaps[s]
        crosses = jnp.logical_and(c < first_doc, c + d >= first_doc)
        return jnp.logical_and(c + d < ctx_width, jnp.logical_not(crosses))

    def takes(s):
        d = gaps[s]
        crosses = jnp.logical_and(c - d < first_doc, c >= first_doc)
        return jnp.logical_and(c - d >= 0, jnp.logical_not(crosses))

    loads = [
        pltpu.make_async_copy(k_in, kv.at[0, 0], load_sem.at[0]),
        pltpu.make_async_copy(v_in, kv.at[0, 1], load_sem.at[1]),
        pltpu.make_async_copy(q_in, q, load_sem.at[2]),
        pltpu.make_async_copy(g_in, g, load_sem.at[3]),
    ]
    for load in loads:
        load.start()

    barrier = pltpu.get_barrier_semaphore()
    expected = jnp.int32(head_width - 1)
    for o in range(1, head_width):
        pl.semaphore_signal(
            barrier, inc=1, device_id=(c, lax.rem(h + o, head_width)), device_id_type=MESH
        )
    for s in range(1, sections):
        for sign, active in ((1, sends(s)), (-1, takes(s))):
            expected = expected + jnp.where(active, parts, 0)

            @pl.when(active)
            def _():
                for xp in range(parts):
                    pl.semaphore_signal(
                        barrier,
                        inc=1,
                        device_id=(c + sign * gaps[s], 2 * xp + kind),
                        device_id_type=MESH,
                    )
    pl.semaphore_wait(barrier, expected)

    def kv_copy(s):
        return remote(
            kv.at[0, kind], kv.at[s, kind], kv_sent.at[s], kv_landed.at[s], c + gaps[s], h
        )

    def pair_copy(s, which):
        return remote(
            kv.at[s, which], kv.at[s, which], pair_sent.at[s], pair_landed.at[s], c, sibling
        )

    loads[0].wait()
    loads[1].wait()
    for s in range(1, sections):
        pl.when(sends(s))(lambda: kv_copy(s).start())
    loads[2].wait()
    loads[3].wait()

    doc_count = lengths.shape[1]
    len_row = lengths[...].astype(F32)
    row_id = lax.broadcasted_iota(jnp.int32, (doc_count, doc_count), 0)
    col_id = lax.broadcasted_iota(jnp.int32, (doc_count, doc_count), 1)
    len_col = jnp.sum(jnp.where(row_id == col_id, len_row, 0.0), axis=1, keepdims=True)
    ends = jnp.sum(jnp.where(row_id <= col_id, len_col, 0.0), axis=0, keepdims=True)
    shift = group.bit_length() - 1
    local_pos = lax.shift_right_logical(
        lax.broadcasted_iota(jnp.int32, (rows, doc_count), 0), shift
    )
    pos = (local_pos + c * tok_rows).astype(F32)
    begin = jnp.max(jnp.where(ends <= pos, ends, 0.0), axis=1, keepdims=True)
    lane = lax.broadcasted_iota(jnp.int32, (block_q, block), 1).astype(F32)
    in_block = lax.shift_right_logical(
        lax.broadcasted_iota(jnp.int32, (block_q, block), 0), shift
    ).astype(F32)
    log_scale = scale * math.log2(math.e)

    def forward(s):
        p = c - gaps[s]
        keys = kv[s, 0]
        values = kv[s, 1]
        with_ones = jnp.concatenate([values, jnp.ones((tok_rows, dim), LOW)], axis=1)
        for i in range(block_count):
            at = pl.ds(i * block_q, block_q)
            raw = dot(q[at], keys, 1, 1)
            tiles = []
            for j in range(block_count):
                tile = raw[:, j * block : (j + 1) * block] * log_scale
                if s == 0 and j > i:
                    tiles.append(jnp.full_like(tile, NEG_FILL))
                    continue
                base = (p * tok_rows + j * block).astype(F32)
                least = begin[i * block_q : (i + 1) * block_q] - base
                least = jnp.where(pattern[i, p * block_count + j] == 1, least, FAR)
                live = lane >= least
                if s == 0 and j == i:
                    live = jnp.logical_and(live, lane <= in_block)
                tiles.append(jnp.where(live, tile, NEG_FILL))
            scores = jnp.concatenate(tiles, axis=1)
            high = jnp.max(scores, axis=1, keepdims=True)
            ex = jnp.exp2(scores - high).astype(LOW)
            e[s, at] = ex
            top[s, at] = jnp.broadcast_to(high, (block_q, dim))
            both = dot(ex, with_ones, 1, 0)
            acc[s, at] = both[:, :dim]
            tot[s, at] = both[:, dim:]
            dp[s, at] = dot(g[at], values, 1, 1)

    forward(0)
    for s in range(1, sections):

        @pl.when(takes(s))
        def _():
            kv_copy(s).wait_recv()
            pair_copy(s, kind).start()

    for s in range(1, sections):
        active = takes(s)

        @pl.when(active)
        def _():
            pair_copy(s, 1 - kind).wait_recv()
            forward(s)

        @pl.when(jnp.logical_not(active))
        def _():
            top[s] = jnp.full((rows, dim), NEG_FILL, F32)
            tot[s] = jnp.zeros((rows, dim), F32)
            acc[s] = jnp.zeros((rows, dim), F32)

    for i in range(block_count):
        at = pl.ds(i * block_q, block_q)
        high = top[0, at]
        for s in range(1, sections):
            high = jnp.maximum(high, top[s, at])
        row_total = jnp.zeros((block_q, dim), F32)
        out = jnp.zeros((block_q, dim), F32)
        weights = []
        for s in range(sections):
            w = jnp.exp2(top[s, at] - high)
            weights.append(w)
            row_total = row_total + w * tot[s, at]
            out = out + w * acc[s, at]
        inverse = 1.0 / row_total
        low = (out * inverse).astype(LOW)
        low_buf[at] = low
        for s in range(sections):
            top[s, at] = weights[s] * inverse
        dots = jnp.sum(g[at].astype(F32) * low.astype(F32), axis=1, keepdims=True)
        mean[at] = jnp.broadcast_to(dots, (block_q, dim))
    o_store = pltpu.make_async_copy(low_buf, o_out, store_sem.at[0])
    o_store.start()

    def swap_copy(s):
        return remote(
            swap_out.at[s], swap_in.at[s], swap_sent.at[s], swap_landed.at[s], c, sibling
        )

    def backward(s):
        for i in range(block_count):
            at = pl.ds(i * block_q, block_q)
            centre = mean[at]
            for j in range(block_count):
                lanes = pl.ds(j * block, block)
                f[s, at, lanes] = (
                    e[s, at, lanes].astype(F32) * (dp[s, at, lanes] - centre)
                ).astype(LOW)
        ratio = top[s]
        q_scaled = (q[...].astype(F32) * (ratio * scale)).astype(LOW)
        g_scaled = (g[...].astype(F32) * ratio).astype(LOW)
        dk = dot(f[s], q_scaled, 0, 0)
        dv = dot(e[s], g_scaled, 0, 0)
        keep[s] = jnp.where(kind == 0, dk, dv)
        swap_out[s] = jnp.where(kind == 0, dv, dk).astype(LOW)
        swap_copy(s).start()

    for s in range(sections - 1, 0, -1):
        pl.when(takes(s))(lambda: backward(s))
    backward(0)

    def flow_copy(s, xp):
        return remote(
            flow_out.at[s, pl.ds(pl.multiple_of(xp * part_rows, 16), part_rows)],
            flow_in.at[s, x],
            flow_sent.at[s, xp],
            flow_landed.at[s, x],
            c - gaps[s],
            2 * xp + kind,
        )

    def flow_wait(s, xs):
        remote(
            flow_out.at[s, pl.ds(0, part_rows)],
            flow_in.at[s, xs],
            flow_sent.at[s, 0],
            flow_landed.at[s, xs],
            c,
            sibling,
        ).wait_recv()

    others = [lax.rem(x + o, parts) for o in range(1, parts)]

    def pass_on(s):
        swap_copy(s).wait_recv()
        joined = keep[s] + swap_in[s].astype(F32)
        if s == 0:
            keep[0] = joined
        flow_out[s] = joined.astype(LOW)
        for xp in range(parts) if s else others:
            flow_copy(s, xp).start()

    for s in range(sections - 1, 0, -1):
        pl.when(takes(s))(lambda: pass_on(s))
    pass_on(0)

    dq_buf[...] = dot(f[0], kv[0, 0], 1, 0) * top[0]
    for s in range(1, sections):

        @pl.when(takes(s))
        def _():
            dq_buf[...] += dot(f[s], kv[s, 0], 1, 0) * top[s]

    o_store.wait()
    low_buf[...] = (dq_buf[...] * scale).astype(LOW)
    dq_store = pltpu.make_async_copy(low_buf, dq_out, store_sem.at[1])
    dq_store.start()

    mine = pl.ds(pl.multiple_of(x * part_rows, 16), part_rows)
    total[...] = keep[0, mine]
    for xs in others:
        flow_wait(0, xs)
        total[...] += flow_in[0, xs].astype(F32)
    for s in range(1, sections):

        @pl.when(sends(s))
        def _():
            for xs in range(parts):
                flow_wait(s, xs)
                total[...] += flow_in[s, xs].astype(F32)

    final[...] = total[...].astype(LOW)

    def fin_copy(out, o):
        return remote(
            final, out.at[mine], fin_sent.at[o], fin_landed.at[o], c, lax.rem(h + o, head_width)
        )

    for which, out in ((0, dk_out), (1, dv_out)):

        @pl.when(kind == which)
        def _():
            for o in range(1, head_width):
                fin_copy(out, o).start()
            own = pltpu.make_async_copy(final, out.at[mine], store_sem.at[2])
            own.start()
            own.wait()

    for o in range(1, head_width):
        source = lax.rem(h + head_width - o, head_width)
        there = pl.ds(pl.multiple_of(lax.div(source, 2) * part_rows, 16), part_rows)
        for which, out in ((0, dk_out), (1, dv_out)):

            @pl.when(lax.rem(source, 2) == which)
            def _():
                remote(
                    final, out.at[there], fin_sent.at[o], fin_landed.at[o], c, source
                ).wait_recv()

    for s in range(1, sections):
        pl.when(sends(s))(lambda: kv_copy(s).wait_send())

        @pl.when(takes(s))
        def _():
            pair_copy(s, kind).wait_send()
            swap_copy(s).wait_send()
            for xp in range(parts):
                flow_copy(s, xp).wait_send()

    swap_copy(0).wait_send()
    for xp in others:
        flow_copy(0, xp).wait_send()
    for o in range(1, head_width):
        fin_copy(dk_out, o).wait_send()
    dq_store.wait()


def local(ctx_width, head_width, queries, key_rows, value_rows, grad_out, doc_lengths, block_pattern):
    tok_rows, group, dim = queries.shape
    rows = tok_rows * group
    sections = ctx_width.bit_length()
    parts = head_width // 2
    part_rows = tok_rows // parts
    anywhere = pl.BlockSpec(memory_space=pl.ANY)
    dma = pltpu.SemaphoreType.DMA
    outs = pl.pallas_call(
        functools.partial(kernel, ctx_width, head_width, group),
        out_shape=(
            jax.ShapeDtypeStruct((rows, dim), LOW),
            jax.ShapeDtypeStruct((rows, dim), LOW),
            jax.ShapeDtypeStruct((tok_rows, dim), LOW),
            jax.ShapeDtypeStruct((tok_rows, dim), LOW),
        ),
        in_specs=[
            pl.BlockSpec(memory_space=pltpu.SMEM),
            pl.BlockSpec(memory_space=pltpu.VMEM),
        ]
        + [anywhere] * 4,
        out_specs=(anywhere,) * 4,
        scratch_shapes=[
            pltpu.VMEM((sections, 2, tok_rows, dim), LOW),
            pltpu.VMEM((rows, dim), LOW),
            pltpu.VMEM((rows, dim), LOW),
            pltpu.VMEM((sections, rows, tok_rows), LOW),
            pltpu.VMEM((sections, rows, tok_rows), LOW),
            pltpu.VMEM((sections, rows, tok_rows), F32),
            pltpu.VMEM((sections, rows, dim), F32),
            pltpu.VMEM((sections, rows, dim), F32),
            pltpu.VMEM((sections, rows, dim), F32),
            pltpu.VMEM((rows, dim), F32),
            pltpu.VMEM((rows, dim), LOW),
            pltpu.VMEM((rows, dim), F32),
            pltpu.VMEM((sections, tok_rows, dim), F32),
            pltpu.VMEM((sections, tok_rows, dim), LOW),
            pltpu.VMEM((sections, tok_rows, dim), LOW),
            pltpu.VMEM((sections, tok_rows, dim), LOW),
            pltpu.VMEM((sections, parts, part_rows, dim), LOW),
            pltpu.VMEM((part_rows, dim), F32),
            pltpu.VMEM((part_rows, dim), LOW),
            dma((4,)),
            dma((3,)),
            dma((sections,)),
            dma((sections,)),
            dma((sections,)),
            dma((sections,)),
            dma((sections,)),
            dma((sections,)),
            dma((sections, parts)),
            dma((sections, parts)),
            dma((head_width,)),
            dma((head_width,)),
        ],
        compiler_params=pltpu.CompilerParams(
            collective_id=0,
            has_side_effects=True,
            vmem_limit_bytes=(12 + 5 * sections) * 1024 * 1024,
        ),
    )(
        block_pattern,
        doc_lengths.reshape(1, -1),
        queries.reshape(rows, dim),
        key_rows,
        value_rows,
        grad_out.reshape(rows, dim),
    )
    attn_out, grad_queries, grad_keys, grad_values = outs
    shape = (tok_rows, group, dim)
    return (attn_out.reshape(shape), grad_queries.reshape(shape), grad_keys, grad_values)


def solution(mesh):
    placed = (
        P("ctx", "head", None),
        P("ctx", None),
        P("ctx", None),
        P("ctx", "head", None),
        P(),
        P("ctx", None),
    )
    return jax.shard_map(
        functools.partial(local, mesh.shape["ctx"], mesh.shape["head"]),
        mesh=mesh,
        in_specs=placed,
        out_specs=(P("ctx", "head", None), P("ctx", "head", None), P("ctx", None), P("ctx", None)),
        check_vma=False,
    )
```

time: 86.4 us -> 38.2 us (0.44)
  the two profiles are of different devices: /device:TPU:0 before, /device:TPU:13 now
where the time goes in v1:
time: 38.2 us; the launch traced here: 38 us
  Pallas kernels  30.4 us (80%)
  local copies, waits for them, and re-layouts  6.94 us (18%)
  between operations  0.66 us (2%)
    pallas_call x1, Pallas kernels, local(): pl.pallas_call(functools.partial(kernel, ctx_width, head_width, group), o...  30.4 us
    unnamed x16, local copies, waits for them, and re-layouts  6.94 us

profile of v1, /device:TPU:13, one launch (start us, length us, event | category | flops | bytes accessed | tf_op | source)
XLA Modules:
  0.0 38.0 jit_solution(17712658710502931983)
XLA Ops:
  0.6 0.0 copy-start.4
  0.6 0.0 copy-start.5
  0.7 0.7 %copy-done.4 = s32[3,24]{1,0:T(4,128)S(1)} copy-done((s32[3,24]{1,0:T(4,128)S(1)}, s32[3,24]{1,0:T(4,128)}, u32[]{:S(2)}) %copy-start.4) | copy-done | bytes 312
  1.3 0.0 copy-done.5
  1.3 0.0 copy-start
  1.3 0.9 %copy-done = bf16[384,2,128]{2,1,0:T(2,128)(2,1)S(1)} copy-done((bf16[384,2,128]{2,1,0:T(2,128)(2,1)S(1)}, bf16[384,2,128]{2,1,0:T(2,128)(2,1)}, u32[]{:S(2)}) %copy-start) | copy-done | bytes 196632
  2.2 0.0 copy-start.1
  2.2 0.9 %copy-done.1 = bf16[384,2,128]{2,1,0:T(2,128)(2,1)S(1)} copy-done((bf16[384,2,128]{2,1,0:T(2,128)(2,1)S(1)}, bf16[384,2,128]{2,1,0:T(2,128)(2,1)}, u32[]{:S(2)}) %copy-start.1) | copy-done | bytes 196632
  3.2 0.0 copy-start.2
  3.2 0.9 %copy-done.2 = bf16[384,128]{1,0:T(8,128)(2,1)S(1)} copy-done((bf16[384,128]{1,0:T(8,128)(2,1)S(1)}, bf16[384,128]{1,0:T(8,128)(2,1)}, u32[]{:S(2)}) %copy-start.2) | copy-done | bytes 98328
  4.1 0.0 copy-start.3
  4.1 0.9 %copy-done.3 = bf16[384,128]{1,0:T(8,128)(2,1)S(1)} copy-done((bf16[384,128]{1,0:T(8,128)(2,1)S(1)}, bf16[384,128]{1,0:T(8,128)(2,1)}, u32[]{:S(2)}) %copy-start.3) | copy-done | bytes 98328
  5.0 30.4 %shard_map.93 = (bf16[768,128]{1,0:T(8,128)(2,1)S(1)}, bf16[768,128]{1,0:T(8,128)(2,1)S(1)}, bf16[384,128]{1,0:T(8,128)(2,1)S(1)}, bf16[384,128]{1,0:T(8,128)(2,1)S(1)}) custom-call(s32[3,24]{1,0:T(4,128)S(1)} %copy-done.4, s32[1,64]{1,0:T(1,128)S(1)} %bitcast.9, bf16[768,128]{1,0:T(8,128)(2,1)S(1)} %bitcast.7, bf16[384,128]{1,0:T(8,128)(2,1)S(1)} %copy-done.2, ...), custom_call_target="tpu_custom_call" | custom-call | tf_op jit(solution)/shard_map/pallas_call | solution.py:352
  35.4 0.7 %copy.14 = bf16[384,2,128]{2,1,0:T(2,128)(2,1)} copy(bf16[384,2,128]{2,1,0:T(2,128)(2,1)S(1)} %bitcast.6) | data formatting | bytes 393216
  36.0 0.7 %copy.15 = bf16[384,2,128]{2,1,0:T(2,128)(2,1)} copy(bf16[384,2,128]{2,1,0:T(2,128)(2,1)S(1)} %bitcast.5) | data formatting | bytes 393216
  36.7 0.6 %copy.16 = bf16[384,128]{1,0:T(8,128)(2,1)} copy(bf16[384,128]{1,0:T(8,128)(2,1)S(1)} %get-tuple-element.18) | data formatting | bytes 196608
  37.3 0.6 %copy.17 = bf16[384,128]{1,0:T(8,128)(2,1)} copy(bf16[384,128]{1,0:T(8,128)(2,1)S(1)} %get-tuple-element.19) | data formatting | bytes 196608
Async XLA Ops:
  0.6 0.7 %copy-start.4 = (s32[3,24]{1,0:T(4,128)S(1)}, s32[3,24]{1,0:T(4,128)}, u32[]{:S(2)}) copy-start(s32[3,24]{1,0:T(4,128)} %pattern.1) | copy-start | bytes 868
  0.6 0.7 %copy-start.5 = (s32[64]{0:T(128)S(1)}, s32[64]{0:T(128)}, u32[]{:S(2)}) copy-start(s32[64]{0:T(128)} %param.10) | copy-start | bytes 772
  1.3 0.9 %copy-start = (bf16[384,2,128]{2,1,0:T(2,128)(2,1)S(1)}, bf16[384,2,128]{2,1,0:T(2,128)(2,1)}, u32[]{:S(2)}) copy-start(bf16[384,2,128]{2,1,0:T(2,128)(2,1)} %param.6) | copy-start | bytes 589828
  2.2 0.9 %copy-start.1 = (bf16[384,2,128]{2,1,0:T(2,128)(2,1)S(1)}, bf16[384,2,128]{2,1,0:T(2,128)(2,1)}, u32[]{:S(2)}) copy-start(bf16[384,2,128]{2,1,0:T(2,128)(2,1)} %param.9) | copy-start | bytes 589828
  3.2 0.9 %copy-start.2 = (bf16[384,128]{1,0:T(8,128)(2,1)S(1)}, bf16[384,128]{1,0:T(8,128)(2,1)}, u32[]{:S(2)}) copy-start(bf16[384,128]{1,0:T(8,128)(2,1)} %k_in.1) | copy-start | bytes 294916
  4.1 0.9 %copy-start.3 = (bf16[384,128]{1,0:T(8,128)(2,1)S(1)}, bf16[384,128]{1,0:T(8,128)(2,1)}, u32[]{:S(2)}) copy-start(bf16[384,128]{1,0:T(8,128)(2,1)} %v_in.1) | copy-start | bytes 294916

commit v2 on v1

--- a/solution.py
+++ b/solution.py
@@ -33,10 +33,10 @@
 
 
 def kernel(
-    ctx_width, head_width, group, pattern, lengths, q_in, k_in, v_in, g_in,
+    ctx_width, head_width, group, pattern_in, lengths_in, q_in, k_in, v_in, g_in,
     o_out, dq_out, dk_out, dv_out,
     kv, q, g, e, f, dp, top, tot, acc, mean, low_buf, dq_buf,
-    keep, swap_out, swap_in, flow_out, flow_in, total, final,
+    keep, swap_out, swap_in, flow_out, flow_in, total, final, pattern, lengths,
     load_sem, store_sem, kv_sent, kv_landed, pair_sent, pair_landed,
     swap_sent, swap_landed, flow_sent, flow_landed, fin_sent, fin_landed,
 ):
@@ -72,6 +72,8 @@
         pltpu.make_async_copy(v_in, kv.at[0, 1], load_sem.at[1]),
         pltpu.make_async_copy(q_in, q, load_sem.at[2]),
         pltpu.make_async_copy(g_in, g, load_sem.at[3]),
+        pltpu.make_async_copy(pattern_in, pattern, load_sem.at[4]),
+        pltpu.make_async_copy(lengths_in, lengths, load_sem.at[5]),
     ]
     for load in loads:
         load.start()
@@ -111,8 +113,8 @@
     loads[1].wait()
     for s in range(1, sections):
         pl.when(sends(s))(lambda: kv_copy(s).start())
-    loads[2].wait()
-    loads[3].wait()
+    for load in loads[2:]:
+        load.wait()
 
     doc_count = lengths.shape[1]
     len_row = lengths[...].astype(F32)
@@ -231,10 +233,6 @@
         swap_out[s] = jnp.where(kind == 0, dv, dk).astype(LOW)
         swap_copy(s).start()
 
-    for s in range(sections - 1, 0, -1):
-        pl.when(takes(s))(lambda: backward(s))
-    backward(0)
-
     def flow_copy(s, xp):
         return remote(
             flow_out.at[s, pl.ds(pl.multiple_of(xp * part_rows, 16), part_rows)],
@@ -267,7 +265,12 @@
             flow_copy(s, xp).start()
 
     for s in range(sections - 1, 0, -1):
-        pl.when(takes(s))(lambda: pass_on(s))
+        pl.when(takes(s))(lambda: backward(s))
+        if s + 1 < sections:
+            pl.when(takes(s + 1))(lambda: pass_on(s + 1))
+    backward(0)
+    if sections > 1:
+        pl.when(takes(1))(lambda: pass_on(1))
     pass_on(0)
 
     dq_buf[...] = dot(f[0], kv[0, 0], 1, 0) * top[0]
@@ -339,6 +342,18 @@
     for o in range(1, head_width):
         fin_copy(dk_out, o).wait_send()
     dq_store.wait()
+
+
+def write_out(*refs):
+    sources, targets, sem = refs[:4], refs[4:8], refs[8]
+    copies = [
+        pltpu.make_async_copy(source, target, sem.at[i])
+        for i, (source, target) in enumerate(zip(sources, targets))
+    ]
+    for copy in copies:
+        copy.start()
+    for copy in copies:
+        copy.wait()
 
 
 def local(ctx_width, head_width, queries, key_rows, value_rows, grad_out, doc_lengths, block_pattern):
@@ -358,10 +373,9 @@
             jax.ShapeDtypeStruct((tok_rows, dim), LOW),
         ),
         in_specs=[
-            pl.BlockSpec(memory_space=pltpu.SMEM),
-            pl.BlockSpec(memory_space=pltpu.VMEM),
+            anywhere,
         ]
-        + [anywhere] * 4,
+        * 6,
         out_specs=(anywhere,) * 4,
         scratch_shapes=[
             pltpu.VMEM((sections, 2, tok_rows, dim), LOW),
@@ -383,7 +397,9 @@
             pltpu.VMEM((sections, parts, part_rows, dim), LOW),
             pltpu.VMEM((part_rows, dim), F32),
             pltpu.VMEM((part_rows, dim), LOW),
-            dma((4,)),
+            pltpu.SMEM(block_pattern.shape, jnp.int32),
+            pltpu.VMEM((1, doc_lengths.shape[0]), jnp.int32),
+            dma((6,)),
             dma((3,)),
             dma((sections,)),
             dma((sections,)),
@@ -399,7 +415,7 @@
         compiler_params=pltpu.CompilerParams(
             collective_id=0,
             has_side_effects=True,
-            vmem_limit_bytes=(12 + 5 * sections) * 1024 * 1024,
+            vmem_limit_bytes=60 * 1024 * 1024,
         ),
     )(
         block_pattern,
@@ -409,6 +425,13 @@
         value_rows,
         grad_out.reshape(rows, dim),
     )
+    outs = pl.pallas_call(
+        write_out,
+        out_shape=tuple(jax.ShapeDtypeStruct(out.shape, out.dtype) for out in outs),
+        in_specs=[pl.BlockSpec(memory_space=pltpu.VMEM)] * 4,
+        out_specs=(anywhere,) * 4,
+        scratch_shapes=[dma((4,))],
+    )(*outs)
     attn_out, grad_queries, grad_keys, grad_values = outs
     shape = (tok_rows, group, dim)
     return (attn_out.reshape(shape), grad_queries.reshape(shape), grad_keys, grad_values)

time: 38.2 us -> 31.3 us (0.82)
  local copies, waits for them, and re-layouts: 6.94 us -> 0 us
    unnamed x16 -> x0, local copies, waits for them, and re-layouts: 6.94 us -> none
    pallas_call x0 -> x1, Pallas kernels: none -> 1.97 us  [local(): pl.pallas_call(write_out, out_shape=tuple((jax.ShapeDtypeStruct(out.shape...]
    pallas_call x1, Pallas kernels: 30.4 us -> 28.5 us  [local(): pl.pallas_call(functools.partial(kernel, ctx_width, head_width, group), o...]
where the time goes in v2:
time: 31.3 us; the launch traced here: 31.1 us
  Pallas kernels  30.5 us (97%)
  between operations  0.64 us (2%)
    pallas_call x1, Pallas kernels, local(): pl.pallas_call(functools.partial(kernel, ctx_width, head_width, group), o...  28.5 us
    pallas_call x1, Pallas kernels, local(): pl.pallas_call(write_out, out_shape=tuple((jax.ShapeDtypeStruct(out.shape...  1.97 us

profile of v2, /device:TPU:13, one launch (start us, length us, event | category | flops | bytes accessed | tf_op | source)
XLA Modules:
  0.0 31.1 jit_solution(13019537799781421633)
XLA Ops:
  0.6 28.5 %shard_map.93 = (bf16[768,128]{1,0:T(8,128)(2,1)}, bf16[768,128]{1,0:T(8,128)(2,1)}, bf16[384,128]{1,0:T(8,128)(2,1)}, bf16[384,128]{1,0:T(8,128)(2,1)}) custom-call(s32[3,24]{1,0:T(4,128)} %pattern_in.1, s32[1,64]{1,0:T(1,128)} %bitcast.7, bf16[768,128]{1,0:T(8,128)(2,1)} %bitcast.5, bf16[384,128]{1,0:T(8,128)(2,1)} %k_in.1, bf16[384,128]{1,0:T(8,128)(2,1)} %v_in.1, ...), custom_call_target="tpu_custom_call" | custom-call | tf_op jit(solution)/shard_map/pallas_call | solution.py:367
  29.2 2.0 %shard_map.94 = (bf16[768,128]{1,0:T(8,128)(2,1)}, bf16[768,128]{1,0:T(8,128)(2,1)}, bf16[384,128]{1,0:T(8,128)(2,1)}, bf16[384,128]{1,0:T(8,128)(2,1)}) custom-call(bf16[768,128]{1,0:T(8,128)(2,1)} %get-tuple-element.12.refs_0_, bf16[768,128]{1,0:T(8,128)(2,1)} %get-tuple-element.13.refs_1_, bf16[384,128]{1,0:T(8,128)(2,1)} %get-tuple-element.14.refs_2_, ...), custom_call_target="tpu_custom_call" | custom-call | tf_op jit(solution)/shard_map/pallas_call | solution.py:428

commit v3 on v2

--- a/solution.py
+++ b/solution.py
@@ -166,14 +166,18 @@
             dp[s, at] = dot(g[at], values, 1, 1)
 
     forward(0)
-    for s in range(1, sections):
-
+
+    def relay(s):
         @pl.when(takes(s))
         def _():
             kv_copy(s).wait_recv()
             pair_copy(s, kind).start()
 
-    for s in range(1, sections):
+    if sections > 1:
+        relay(1)
+    for s in range(1, sections):
+        if s + 1 < sections:
+            relay(s + 1)
         active = takes(s)
 
         @pl.when(active)
@@ -261,7 +265,7 @@
         if s == 0:
             keep[0] = joined
         flow_out[s] = joined.astype(LOW)
-        for xp in range(parts) if s else others:
+        for xp in others + [x] if s else others:
             flow_copy(s, xp).start()
 
     for s in range(sections - 1, 0, -1):

time: 31.3 us -> 30.3 us (0.968)
  Pallas kernels: 30.5 us -> 29.5 us
    pallas_call x1, Pallas kernels: 28.5 us -> 27.5 us  [local(): pl.pallas_call(functools.partial(kernel, ctx_width, head_width, group), o...]
where the time goes in v3:
time: 30.3 us; the launch traced here: 30.1 us
  Pallas kernels  29.5 us (97%)
  between operations  0.64 us (2%)
    pallas_call x1, Pallas kernels, local(): pl.pallas_call(functools.partial(kernel, ctx_width, head_width, group), o...  27.5 us
    pallas_call x1, Pallas kernels, local(): pl.pallas_call(write_out, out_shape=tuple((jax.ShapeDtypeStruct(out.shape...  1.97 us

profile of v3, /device:TPU:13, one launch (start us, length us, event | category | flops | bytes accessed | tf_op | source)
XLA Modules:
  0.0 30.1 jit_solution(11422709696498516440)
XLA Ops:
  0.6 27.5 %shard_map.93 = (bf16[768,128]{1,0:T(8,128)(2,1)}, bf16[768,128]{1,0:T(8,128)(2,1)}, bf16[384,128]{1,0:T(8,128)(2,1)}, bf16[384,128]{1,0:T(8,128)(2,1)}) custom-call(s32[3,24]{1,0:T(4,128)} %pattern_in.1, s32[1,64]{1,0:T(1,128)} %bitcast.7, bf16[768,128]{1,0:T(8,128)(2,1)} %bitcast.5, bf16[384,128]{1,0:T(8,128)(2,1)} %k_in.1, bf16[384,128]{1,0:T(8,128)(2,1)} %v_in.1, ...), custom_call_target="tpu_custom_call" | custom-call | tf_op jit(solution)/shard_map/pallas_call | solution.py:371
  28.2 2.0 %shard_map.94 = (bf16[768,128]{1,0:T(8,128)(2,1)}, bf16[768,128]{1,0:T(8,128)(2,1)}, bf16[384,128]{1,0:T(8,128)(2,1)}, bf16[384,128]{1,0:T(8,128)(2,1)}) custom-call(bf16[768,128]{1,0:T(8,128)(2,1)} %get-tuple-element.12.refs_0_, bf16[768,128]{1,0:T(8,128)(2,1)} %get-tuple-element.13.refs_1_, bf16[384,128]{1,0:T(8,128)(2,1)} %get-tuple-element.14.refs_2_, ...), custom_call_target="tpu_custom_call" | custom-call | tf_op jit(solution)/shard_map/pallas_call | solution.py:432
